TPU v7x, 256 devices: a whole 4x4x8 slice. The times are simulated.
256 devices in a mesh: seq: 128 (over x, y, z), head: 2 (over core).
Axes of the slice: x: 4, y: 4, z: 8, core: 2. Of those that a mesh axis runs over, the one named last changes fastest.
Arguments:
- query_rows: bfloat16 [65536, 1024], P('seq', 'head'), may hold values from -16 to 16
- key_rows: bfloat16 [65536, 1024], P('seq', 'head'), may hold values from -16 to 16
- value_rows: bfloat16 [65536, 1024], P('seq', 'head'), may hold values from -16 to 16
- segment_lengths: int32 [256], replicated, may hold values from 1 to 512, 65536 in all
Outputs:
- attended: bfloat16 [65536, 1024], P('seq', 'head')
Inputs may be any that keep to these rules, and one draw needn't show every extreme that they name: `segment_lengths`: they sum to 65536; the largest is exactly 512.
All inputs are finite; a program needn't handle non-finite values.
Results may differ from a plain program's by a relative error of at most 0.0065.
Values may be sent and summed in bfloat16 or wider, within the bound.
A program may use at most 192 MiB of HBM per device.

v0:
```python
import math

import jax
import jax.numpy as jnp
from jax import lax
from jax.sharding import PartitionSpec as P

HEAD_DIM = 128
ITERS = 6


def newton(attention_kernel, peak):
    eye = jnp.eye(attention_kernel.shape[-1], dtype=jnp.float32)
    high = lax.Precision.HIGHEST
    inverse = jnp.swapaxes(attention_kernel, -1, -2) / peak
    for step in range(ITERS):
        prod = jnp.matmul(attention_kernel, inverse, precision=high)
        inner = 7.0 * eye - prod
        inner = 15.0 * eye - jnp.matmul(prod, inner, precision=high)
        inner = 13.0 * eye - jnp.matmul(prod, inner, precision=high)
        inverse = 0.25 * jnp.matmul(inverse, inner, precision=high)
    return inverse


def per_device(query_rows, key_rows, value_rows, segment_lengths):
    tok_dev = query_rows.shape[0]
    features = query_rows.shape[1]
    heads_dev = features // HEAD_DIM
    landmarks = segment_lengths.shape[0]
    score_scale = 1.0 / math.sqrt(HEAD_DIM)
    ends = jnp.cumsum(segment_lengths)
    starts = ends - segment_lengths
    shard_start = lax.axis_index("seq") * tok_dev
    position = shard_start + lax.iota(jnp.int32, tok_dev)
    member = ((position[:, None] >= starts[None, :]) & (position[:, None] < ends[None, :])).astype(
        jnp.bfloat16
    )
    query_sum = jnp.einsum("tm,tf->mf", member, query_rows, preferred_element_type=jnp.float32)
    key_sum = jnp.einsum("tm,tf->mf", member, key_rows, preferred_element_type=jnp.float32)
    counts = segment_lengths.astype(jnp.float32)[:, None]
    query_sum, key_sum = lax.psum((query_sum, key_sum), "seq")
    query_land = (query_sum / counts).astype(jnp.bfloat16)
    key_land = (key_sum / counts).astype(jnp.bfloat16)
    landmark_query = query_land.reshape(landmarks, heads_dev, HEAD_DIM)
    landmark_key = key_land.reshape(landmarks, heads_dev, HEAD_DIM)
    query_head_stack = query_rows.reshape(tok_dev, heads_dev, HEAD_DIM)
    key_head_stack = key_rows.reshape(tok_dev, heads_dev, HEAD_DIM)
    value_head_stack = value_rows.reshape(tok_dev, heads_dev, HEAD_DIM)
    score = (
        jnp.einsum(
            "ozc,uzc->zou", landmark_query, key_head_stack, preferred_element_type=jnp.float32
        )
        * score_scale
    )
    local_top = jnp.max(score, axis=-1)
    attention_weight = jnp.exp(score - local_top[..., None])
    local_total = jnp.sum(attention_weight, axis=-1)
    local_numer = jnp.einsum(
        "cqn,nco->cqo",
        attention_weight.astype(jnp.bfloat16),
        value_head_stack,
        preferred_element_type=jnp.float32,
    )
    highest = lax.pmax(local_top, "seq")
    factor = jnp.exp(local_top - highest)
    total, numer = lax.psum((local_total * factor, local_numer * factor[..., None]), "seq")
    keyside = numer / total[..., None]
    attention_kernel = jax.nn.softmax(
        jnp.einsum("qfz,yfz->fqy", landmark_query, landmark_key, preferred_element_type=jnp.float32)
        * score_scale,
        axis=-1,
    )
    local_peak = jnp.max(jnp.sum(attention_kernel, axis=1))
    peak = lax.pmax(local_peak, "head")
    inverse = newton(attention_kernel, peak)
    pseudo_inverse_mixer = jnp.matmul(inverse, keyside, precision=lax.Precision.HIGHEST).astype(
        jnp.bfloat16
    )
    token_score = (
        jnp.einsum(
            "xuq,luq->uxl", query_head_stack, landmark_key, preferred_element_type=jnp.float32
        )
        * score_scale
    )
    token_landmark_weight = jax.nn.softmax(token_score, axis=-1).astype(jnp.bfloat16)
    attended = jnp.einsum(
        "gzj,gjs->zgs",
        token_landmark_weight,
        pseudo_inverse_mixer,
        preferred_element_type=jnp.float32,
    )
    return attended.astype(jnp.bfloat16).reshape(tok_dev, features)


def solution(mesh):
    in_specs = (P("seq", "head"), P("seq", "head"), P("seq", "head"), P())
    out_specs = P("seq", "head")
    return jax.shard_map(
        per_device, mesh=mesh, in_specs=in_specs, out_specs=out_specs, check_vma=False
    )
```

profile of v0, /device:TPU:1, one launch (start us, length us, event | category | flops | bytes accessed | tf_op | source)
XLA Modules:
  0.0 1007.1 jit_solution(12734227871936861875)
XLA Ops:
  6.5 1.0 reduce-window.9
  7.7 0.1 slice_reduce_fusion
  7.8 0.8 fusion.90
  8.6 2.3 fusion.61
  11.0 1.2 fusion.60
  12.2 216.1 %all-reduce.4.cloned.1.call-done = f32[256,512]{1,0:T(8,128)} async-done(((f32[256,512]{1,0:T(8,128)}), f32[256,512]{1,0:T(8,128)}) %all-reduce.4.cloned.1.call-update) | async-done | bytes 524304 | tf_op jit(solution)/shard_map/psum | solution.py:41
  228.3 1.7 multiply_reduce_fusion
  230.0 291.7 %pmax.15 = f32[4,256]{1,0:T(4,128)S(1)} all-reduce(f32[4,256]{1,0:T(4,128)S(1)} %get-tuple-element.12), channel_id=1, replica_groups=mesh['seq'=128,'head'=2] {'seq'}, use_global_device_ids=true, to_apply=%region_10.11 | all-reduce | flops 1024 | bytes 8192 | tf_op jit(solution)/shard_map/pmax | solution.py:64
  521.7 0.6 fusion.6
  522.3 1.5 convolution_multiply_fusion.7
  523.9 287.0 %psum.31 = f32[4,256]{1,0:T(4,128)S(1)} all-reduce(f32[4,256]{1,0:T(4,128)S(1)} %get-tuple-element.7), channel_id=1, replica_groups=mesh['seq'=128,'head'=2] {'seq'}, use_global_device_ids=true, to_apply=%region_13.14 | all-reduce | flops 1024 | bytes 8192 | tf_op jit(solution)/shard_map/psum | solution.py:66
  810.8 1.7 fusion.91
  812.6 0.4 fusion.44
  813.0 0.4 fusion.66
  813.3 0.6 reduce_max.37
  813.9 0.2 copy-done.14
  814.1 1.8 fusion.45
  816.0 118.7 %pmax.14 = f32[]{:T(128)} all-reduce(f32[]{:T(128)} %reduce_max.37), channel_id=1, replica_groups=mesh['seq'=128,'head'=2] {'head'}, use_global_device_ids=true, to_apply=%region_8.9 | all-reduce | flops 1 | bytes 8 | tf_op jit(solution)/shard_map/pmax | solution.py:74
  934.6 0.6 broadcast_multiply_fusion
  935.3 1.8 fusion.63
  937.1 1.2 fusion.20
  938.3 1.2 convolution_subtract_fusion.5
  939.5 3.2 convolution_multiply_fusion.5
  942.6 4.6 online-softmax
  947.3 2.8 fusion.23
  950.1 1.2 convolution_subtract_fusion.4
  951.3 2.1 convolution_multiply_fusion.4
  953.4 4.6 online-softmax.1
  958.1 2.8 fusion.26
  960.9 1.2 convolution_subtract_fusion.3
  962.1 2.1 convolution_multiply_fusion.3
  964.3 4.6 online-softmax.2
  968.9 2.8 fusion.29
  971.7 1.2 convolution_subtract_fusion.2
  972.9 2.1 convolution_multiply_fusion.2
  975.1 4.6 online-softmax.3
  979.7 2.8 fusion.32
  982.5 1.2 convolution_subtract_fusion.1
  983.8 2.1 convolution_multiply_fusion.1
  985.9 4.6 online-softmax.4
  990.5 2.8 fusion.35
  993.4 1.2 convolution_subtract_fusion
  994.6 1.1 convolution_multiply_fusion
  995.7 0.4 copy-done.11
  996.2 1.6 fusion.92
  997.7 1.2 convolution_convert_fusion.1
  998.9 0.3 convolution_convert_fusion
  999.3 1.0 copy.36
  (43 shorter events, 0.6 us)
Async XLA Ops:
  6.5 4.5 copy-start
  6.5 221.8 %all-reduce.4.cloned.1.call-start = ((), (), s32[]{:S(2)}) async-start(), calls=%async_computation | async-start | bytes 1048576 | tf_op jit(solution)/shard_map/psum | solution.py:41
  11.0 799.9 %all-reduce.6.cloned.1.call-start = ((), (), s32[]{:S(2)}) async-start(), calls=%async_computation.1 | async-start | bytes 2097152 | tf_op jit(solution)/shard_map/psum | solution.py:41
  228.3 294.0 %copy-start.15 = (bf16[512,512]{1,0:T(8,128)(2,1)S(1)}, bf16[512,512]{1,0:T(8,128)(2,1)}, u32[]{:S(2)}) copy-start(bf16[512,512]{1,0:T(8,128)(2,1)} %param.6) | copy-start | bytes 1572868
  812.5 126.9 %copy-start.1 = (f32[4,256,256]{2,1,0:T(8,128)}, f32[4,256,256]{2,1,0:T(8,128)S(1)}, u32[]{:S(2)}) copy-start(f32[4,256,256]{2,1,0:T(8,128)S(1)} %get-tuple-element.15) | copy-start | bytes 3145732
  812.5 1.4 copy-start.13
  812.6 1.6 copy-start.14
  947.3 2.8 copy-start.3
  950.1 1.2 copy-start.12
  958.1 2.8 copy-start.4
  960.9 1.2 copy-start.8
  968.9 2.8 copy-start.5
  971.7 1.2 copy-start.9
  979.7 2.8 copy-start.6
  982.5 1.2 copy-start.10
  990.5 2.8 copy-start.2
  993.3 1.2 copy-start.7
  994.6 1.6 copy-start.11
  996.2 1.6 copy-start.16
Sparse Core Ops, SparseCore 0:
  12.8 215.5 all-reduce.3
  523.9 267.7 all-reduce.5
where the time goes:
time: 1010 us
  blocking collectives  697 us (69%)
  waiting for transfers between devices  216 us (21%)
  matrix products  48.5 us (5%)
  Pallas kernels  23.2 us (2%)
  between operations  13.7 us (1%)
    pmax x1, blocking collectives, per_device(): highest = lax.pmax(local_top, 'seq')  292 us
    psum x1, blocking collectives, per_device(): lax.psum((local_total * factor, local_numer * factor[..., None]), 'seq')  287 us
    psum x2, waiting for transfers between devices, per_device(): query_sum, key_sum = lax.psum((query_sum, key_sum), 'seq')  216 us
    pmax x1, blocking collectives, per_device(): peak = lax.pmax(local_peak, 'head')  119 us
    unnamed x5, Pallas kernels  23.2 us
  transfers between devices with their start and end apart: 2, of which 1 were waited for; matrix products, arithmetic and copies ran while one was open for 0% of the time, Pallas kernels for 0%

commit v1 on v0

v1 whole, which is shorter than its diff:
```python
import functools
import math

import jax
import jax.numpy as jnp
from jax import lax
from jax.experimental import pallas as pl
from jax.experimental.pallas import tpu as pltpu
from jax.sharding import PartitionSpec as P

HEAD_DIM = 128
ITERS = 6
MESH = pl.DeviceIdType.MESH
F32 = jnp.float32
BF16 = jnp.bfloat16
HIGH = lax.Precision.HIGHEST


def nt(a, b, precision=None):
    return lax.dot_general(
        a, b, (((1,), (1,)), ((), ())), precision=precision, preferred_element_type=F32
    )


def nn(a, b, precision=None):
    return lax.dot_general(
        a, b, (((1,), (0,)), ((), ())), precision=precision, preferred_element_type=F32
    )


class Exchange:
    def __init__(self, n, me, seq_of, src, dst, send_sem, recv_sem):
        self.n, self.me, self.seq_of = n, me, seq_of
        self.src, self.dst = src, dst
        self.send_sem, self.recv_sem = send_sem, recv_sem

    def copy(self, partner, slot):
        return pltpu.make_async_remote_copy(
            src_ref=self.src(partner),
            dst_ref=self.dst(slot),
            send_sem=self.send_sem.at[partner],
            recv_sem=self.recv_sem.at[slot],
            device_id={"seq": self.seq_of(partner)},
            device_id_type=MESH,
        )

    def each(self, act):
        def body(i, carry):
            act(lax.rem(self.me + i, self.n))
            return carry

        lax.fori_loop(1, self.n, body, 0)

    def start(self):
        self.each(lambda p: self.copy(p, self.me).start())

    def start_one(self, p):
        @pl.when(p != self.me)
        def _():
            self.copy(p, self.me).start()

    def wait_recv(self):
        self.each(lambda p: self.copy(p, p).wait_recv())

    def wait_send(self):
        self.each(lambda p: self.copy(p, self.me).wait_send())


def kernel(
    n_plane, n_z,
    lens_ref, q_ref, k_ref, v_ref, out_ref,
    tail, sums_send, sums_recv, z_send, z_recv, land, peaks,
    numer_send, numer_recv, numer_z_send, numer_z_recv, mixer_z, mixer,
    kernel_ref, kernel_t, inv_ref, tok_weight,
    tail_sem, peak_sem,
    a_send, a_recv, b_send, b_recv, c_send, c_recv, d_send, d_recv,
    e_send, e_recv, f_send, f_recv, g_send, g_recv, h_send, h_recv,
):
    n_seq = n_plane * n_z
    toks, feats = q_ref.shape
    heads = feats // HEAD_DIM
    marks = lens_ref.shape[1]
    scale = 1.0 / math.sqrt(HEAD_DIM)
    mark_part = marks // n_plane
    col_part = 2 * feats // n_z
    row_part = feats // n_plane
    row_z = row_part // n_z
    parts_head = n_plane // heads

    seq = lax.axis_index("seq")
    head = lax.axis_index("head")
    plane, z = seq // n_z, lax.rem(seq, n_z)
    after, before = lax.rem(seq + 1, n_seq), lax.rem(seq + n_seq - 1, n_seq)

    def plane_seq(p):
        return p * n_z + z

    def z_seq(p):
        return plane * n_z + p

    barrier = pltpu.get_barrier_semaphore()

    def greet(**where):
        pl.semaphore_signal(barrier, inc=1, device_id=where, device_id_type=MESH)

    def greet_plane(i, carry):
        greet(seq=plane_seq(lax.rem(plane + i, n_plane)))
        return carry

    def greet_z(i, carry):
        greet(seq=z_seq(lax.rem(z + i, n_z)))
        return carry

    lax.fori_loop(1, n_plane, greet_plane, 0)
    lax.fori_loop(1, n_z, greet_z, 0)
    greet(seq=after)
    greet(seq=before)
    greet(head=1 - head)

    lens = lens_ref[...].astype(F32)
    row = lax.broadcasted_iota(jnp.int32, (marks, marks), 0)
    col = lax.broadcasted_iota(jnp.int32, (marks, marks), 1)
    counts = jnp.sum(jnp.where(col == row, lens, 0.0), axis=1, keepdims=True)
    ends = jnp.sum(jnp.where(col <= row, lens, 0.0), axis=1, keepdims=True)
    starts = ends - counts
    base = (seq * toks).astype(F32)
    top_pos = base + toks
    runs_on = (starts < top_pos) & (ends > top_pos)
    came_in = (starts < base) & (ends > base)
    run_start = top_pos + jnp.sum(jnp.where(runs_on, starts - top_pos, 0.0), axis=0, keepdims=True)

    pos8 = base + lax.broadcasted_iota(jnp.int32, (8, toks), 1).astype(F32)
    tail_member = jnp.where(pos8 >= run_start, 1.0, 0.0).astype(BF16)
    row8 = lax.broadcasted_iota(jnp.int32, (8, HEAD_DIM), 0)
    blocks = 2 * heads
    packed = jnp.zeros((8, HEAD_DIM), F32)
    for half, ref in enumerate((q_ref, k_ref)):
        sums = nn(tail_member, ref[...])
        for h in range(heads):
            packed = jnp.where(
                row8 == half * heads + h, sums[:, h * HEAD_DIM:(h + 1) * HEAD_DIM], packed
            )
    tail[0] = packed

    pl.semaphore_wait(barrier, (n_plane - 1) + (n_z - 1) + 3)
    tail_copy = pltpu.make_async_remote_copy(
        src_ref=tail.at[0], dst_ref=tail.at[1], send_sem=tail_sem.at[0], recv_sem=tail_sem.at[1],
        device_id={"seq": after}, device_id_type=MESH,
    )
    tail_copy.start()

    pos = base + lax.broadcasted_iota(jnp.int32, (marks, toks), 1).astype(F32)
    member = jnp.where((pos >= starts) & (pos < ends), 1.0, 0.0).astype(BF16)
    sums = [nn(member, q_ref[...]), nn(member, k_ref[...])]
    tail_copy.wait_recv()
    for b in range(blocks):
        s = sums[b // heads]
        o = (b % heads) * HEAD_DIM
        block = s[:, o:o + HEAD_DIM] + jnp.where(came_in, tail[1, b:b + 1, :], 0.0)
        block = jnp.where(runs_on, 0.0, block / counts).astype(BF16)
        sums_send[:, :, b * HEAD_DIM:(b + 1) * HEAD_DIM] = block.reshape(
            n_plane, mark_part, HEAD_DIM
        )

    ex_a = Exchange(n_plane, plane, plane_seq, lambda p: sums_send.at[p], lambda p: sums_recv.at[p],
                    a_send, a_recv)
    ex_a.start()
    sums_recv[plane] = sums_send[plane]
    ex_a.wait_recv()
    part = sums_recv[0].astype(F32)
    for p in range(1, n_plane):
        part = part + sums_recv[p].astype(F32)
    part = part.astype(BF16)
    for p in range(n_z):
        z_send[p] = part[:, p * col_part:(p + 1) * col_part]

    ex_b = Exchange(n_z, z, z_seq, lambda p: z_send.at[p], lambda p: z_recv.at[p], b_send, b_recv)
    ex_b.start()
    z_recv[z] = z_send[z]
    ex_b.wait_recv()
    part = z_recv[0].astype(F32)
    for p in range(1, n_z):
        part = part + z_recv[p].astype(F32)
    land[plane, z] = part.astype(BF16)

    ex_c = Exchange(n_z, z, z_seq, lambda p: land.at[plane, z], lambda p: land.at[plane, p],
                    c_send, c_recv)
    ex_c.start()
    ex_c.wait_recv()
    ex_d = Exchange(n_plane, plane, plane_seq, lambda p: land.at[plane], lambda p: land.at[p],
                    d_send, d_recv)
    ex_d.start()
    ex_d.wait_recv()

    def landmark(b):
        where, off = (b * HEAD_DIM) // col_part, (b * HEAD_DIM) % col_part
        return land[:, where, :, off:off + HEAD_DIM].reshape(marks, HEAD_DIM)

    my_head = plane // parts_head
    peak = jnp.zeros((1, 1), F32)
    for h in range(heads):
        score = nt(landmark(h), landmark(heads + h)) * scale
        weight = jnp.exp(score - jnp.max(score, axis=1, keepdims=True))
        soft = weight / jnp.sum(weight, axis=1, keepdims=True)
        column = jnp.sum(soft, axis=0, keepdims=True)
        peak = jnp.maximum(peak, jnp.max(column, axis=1, keepdims=True))

        @pl.when(my_head == h)
        def _():
            kernel_ref[...] = soft

    peaks[0] = jnp.broadcast_to(peak, (8, HEAD_DIM))
    peak_copy = pltpu.make_async_remote_copy(
        src_ref=peaks.at[0], dst_ref=peaks.at[1], send_sem=peak_sem.at[0], recv_sem=peak_sem.at[1],
        device_id={"head": 1 - head}, device_id_type=MESH,
    )
    peak_copy.start()

    ex_e = Exchange(n_plane, plane, plane_seq, lambda p: numer_send.at[p],
                    lambda p: numer_recv.at[p], e_send, e_recv)
    pad = numer_send.shape[1] - row_part - 2
    for h in range(heads):
        cols = slice(h * HEAD_DIM, (h + 1) * HEAD_DIM)
        score = nt(k_ref[:, cols], landmark(h)) * scale
        top = jnp.max(score, axis=0, keepdims=True)
        weight = jnp.exp(score - top)
        total = jnp.sum(weight, axis=0, keepdims=True)
        numer = lax.dot_general(
            v_ref[:, cols], weight.astype(BF16), (((0,), (0,)), ((), ())),
            preferred_element_type=F32,
        )
        for j in range(parts_head):
            p = h * parts_head + j
            numer_send[p, :row_part, :] = numer[j * row_part:(j + 1) * row_part]
            numer_send[p, row_part:row_part + 1, :] = top
            numer_send[p, row_part + 1:row_part + 2, :] = total
            numer_send[p, row_part + 2:, :] = jnp.zeros((pad, marks), F32)
            ex_e.start_one(p)
    numer_recv[plane] = numer_send[plane]

    kernel_t[...] = kernel_ref[...].T
    peak_copy.wait_recv()
    peak = jnp.maximum(peaks[0, 0:1, 0:1], peaks[1, 0:1, 0:1])
    inv_ref[...] = kernel_ref[...] / peak

    def newton(step, carry):
        inv = inv_ref[...]
        prod = nn(inv, kernel_t[...], HIGH)
        square = nn(prod, prod, HIGH)
        once = nn(prod, inv, HIGH)
        rest = nn(7.0 * prod - square, once, HIGH)
        inv_ref[...] = 0.25 * (13.0 * inv - 15.0 * once + rest)
        return carry

    lax.fori_loop(0, ITERS // 2, newton, 0)

    def merge(ref, count, rows):
        tops = [ref[p, rows:rows + 1, :] for p in range(count)]
        high = functools.reduce(jnp.maximum, tops)
        numer, total = None, None
        for p in range(count):
            factor = jnp.exp(tops[p] - high)
            n, t = factor * ref[p, :rows, :], factor * ref[p, rows + 1:rows + 2, :]
            numer, total = (n, t) if numer is None else (numer + n, total + t)
        return numer, total, high

    ex_e.wait_recv()
    numer, total, high = merge(numer_recv, n_plane, row_part)
    pad = numer_z_send.shape[1] - row_z - 2
    for p in range(n_z):
        numer_z_send[p, :row_z, :] = numer[p * row_z:(p + 1) * row_z]
        numer_z_send[p, row_z:row_z + 1, :] = high
        numer_z_send[p, row_z + 1:row_z + 2, :] = total
        numer_z_send[p, row_z + 2:, :] = jnp.zeros((pad, marks), F32)
    ex_f = Exchange(n_z, z, z_seq, lambda p: numer_z_send.at[p], lambda p: numer_z_recv.at[p],
                    f_send, f_recv)
    ex_f.start()
    numer_z_recv[z] = numer_z_send[z]

    lax.fori_loop(ITERS // 2, ITERS, newton, 0)

    ex_f.wait_recv()
    numer, total, high = merge(numer_z_recv, n_z, row_z)
    keyside = numer / total
    rows_z = mixer_z.shape[1]
    if rows_z > row_z:
        keyside = jnp.concatenate([keyside, jnp.zeros((rows_z - row_z, marks), F32)], axis=0)
    mixer_z[z] = nn(keyside, inv_ref[...], HIGH)
    ex_g = Exchange(n_z, z, z_seq, lambda p: mixer_z.at[z], lambda p: mixer_z.at[p], g_send, g_recv)
    ex_g.start()

    def token_side(h):
        score = nt(q_ref[:, h * HEAD_DIM:(h + 1) * HEAD_DIM], landmark(heads + h)) * scale
        weight = jnp.exp(score - jnp.max(score, axis=1, keepdims=True))
        tok_weight[h] = (weight / jnp.sum(weight, axis=1, keepdims=True)).astype(BF16)

    for h in range(heads // 2):
        token_side(h)
    ex_g.wait_recv()
    mixer[plane] = jnp.concatenate([mixer_z[p, :row_z, :] for p in range(n_z)], axis=0).astype(BF16)
    ex_h = Exchange(n_plane, plane, plane_seq, lambda p: mixer.at[plane], lambda p: mixer.at[p],
                    h_send, h_recv)
    ex_h.start()
    for h in range(heads // 2, heads):
        token_side(h)
    ex_h.wait_recv()
    for h in range(heads):
        mix = mixer[h * parts_head:(h + 1) * parts_head].reshape(HEAD_DIM, marks)
        out_ref[:, h * HEAD_DIM:(h + 1) * HEAD_DIM] = nt(tok_weight[h], mix).astype(BF16)

    tail_copy.wait_send()
    peak_copy.wait_send()
    for ex in (ex_a, ex_b, ex_c, ex_d, ex_e, ex_f, ex_g, ex_h):
        ex.wait_send()


def per_device(n_plane, n_z, query_rows, key_rows, value_rows, segment_lengths):
    toks, feats = query_rows.shape
    marks = segment_lengths.shape[0]
    heads = feats // HEAD_DIM
    mark_part, col_part = marks // n_plane, 2 * feats // n_z
    row_part = feats // n_plane
    row_z = row_part // n_z
    up = lambda n: -(-n // 8) * 8
    dma = pltpu.SemaphoreType.DMA
    return pl.pallas_call(
        functools.partial(kernel, n_plane, n_z),
        out_shape=jax.ShapeDtypeStruct((toks, feats), BF16),
        in_specs=[pl.BlockSpec(memory_space=pltpu.VMEM)] * 4,
        out_specs=pl.BlockSpec(memory_space=pltpu.VMEM),
        scratch_shapes=[
            pltpu.VMEM((2, 8, HEAD_DIM), F32),
            pltpu.VMEM((n_plane, mark_part, 2 * feats), BF16),
            pltpu.VMEM((n_plane, mark_part, 2 * feats), BF16),
            pltpu.VMEM((n_z, mark_part, col_part), BF16),
            pltpu.VMEM((n_z, mark_part, col_part), BF16),
            pltpu.VMEM((n_plane, n_z, mark_part, col_part), BF16),
            pltpu.VMEM((2, 8, HEAD_DIM), F32),
            pltpu.VMEM((n_plane, up(row_part + 2), marks), F32),
            pltpu.VMEM((n_plane, up(row_part + 2), marks), F32),
            pltpu.VMEM((n_z, up(row_z + 2), marks), F32),
            pltpu.VMEM((n_z, up(row_z + 2), marks), F32),
            pltpu.VMEM((n_z, up(row_z), marks), F32),
            pltpu.VMEM((n_plane, row_part, marks), BF16),
            pltpu.VMEM((marks, marks), F32),
            pltpu.VMEM((marks, marks), F32),
            pltpu.VMEM((marks, marks), F32),
            pltpu.VMEM((heads, toks, marks), BF16),
            dma((2,)),
            dma((2,)),
        ] + [dma((n,)) for n in (n_plane, n_z, n_z, n_plane, n_plane, n_z, n_z, n_plane) for _ in range(2)],
        compiler_params=pltpu.CompilerParams(
            collective_id=0, has_side_effects=True, vmem_limit_bytes=48 * 1024 * 1024
        ),
    )(segment_lengths.reshape(1, marks), query_rows, key_rows, value_rows)


def solution(mesh):
    n_seq = mesh.shape["seq"]
    n_z = 8 if n_seq >= 128 else 2
    in_specs = (P("seq", "head"), P("seq", "head"), P("seq", "head"), P())
    return jax.shard_map(
        functools.partial(per_device, n_seq // n_z, n_z),
        mesh=mesh, in_specs=in_specs, out_specs=P("seq", "head"), check_vma=False,
    )
```

time: 1010 us -> 74.1 us (0.07)
  the two profiles are of different devices: /device:TPU:1 before, /device:TPU:8 now
where the time goes in v1:
time: 74.1 us; the launch traced here: 73.8 us
  Pallas kernels  69.2 us (93%)
  local copies, waits for them, and re-layouts  4.6 us (6%)
    pallas_call x1, Pallas kernels, per_device(): pl.pallas_call(functools.partial(kernel, n_plane, n_z), out_shape=jax.Sha...  69.2 us
    unnamed x9, local copies, waits for them, and re-layouts  4.6 us

profile of v1, /device:TPU:8, one launch (start us, length us, event | category | flops | bytes accessed | tf_op | source)
XLA Modules:
  0.0 73.8 jit_solution(5748463465191894375)
XLA Ops:
  0.0 0.0 copy-start.3
  0.0 0.7 copy-done.3
  0.7 0.0 copy-start
  0.7 1.0 %copy-done = bf16[512,512]{1,0:T(8,128)(2,1)S(1)} copy-done((bf16[512,512]{1,0:T(8,128)(2,1)S(1)}, bf16[512,512]{1,0:T(8,128)(2,1)}, u32[]{:S(2)}) %copy-start) | copy-done | bytes 524312
  1.7 0.0 copy-start.1
  1.7 1.0 %copy-done.1 = bf16[512,512]{1,0:T(8,128)(2,1)S(1)} copy-done((bf16[512,512]{1,0:T(8,128)(2,1)S(1)}, bf16[512,512]{1,0:T(8,128)(2,1)}, u32[]{:S(2)}) %copy-start.1) | copy-done | bytes 524312
  2.8 0.0 copy-start.2
  2.8 1.0 %copy-done.2 = bf16[512,512]{1,0:T(8,128)(2,1)S(1)} copy-done((bf16[512,512]{1,0:T(8,128)(2,1)S(1)}, bf16[512,512]{1,0:T(8,128)(2,1)}, u32[]{:S(2)}) %copy-start.2) | copy-done | bytes 524312
  3.8 69.2 %shard_map.46 = bf16[512,512]{1,0:T(8,128)(2,1)S(1)} custom-call(s32[1,256]{1,0:T(1,128)S(1)} %bitcast.1, bf16[512,512]{1,0:T(8,128)(2,1)S(1)} %copy-done, bf16[512,512]{1,0:T(8,128)(2,1)S(1)} %copy-done.1, bf16[512,512]{1,0:T(8,128)(2,1)S(1)} %copy-done.2), custom_call_target="tpu_custom_call" | custom-call | tf_op jit(solution)/shard_map/pallas_call | solution.py:326
  73.0 0.8 %copy.6 = bf16[512,512]{1,0:T(8,128)(2,1)} copy(bf16[512,512]{1,0:T(8,128)(2,1)S(1)} %shard_map.46) | data formatting | bytes 1048576
Async XLA Ops:
  0.0 0.7 copy-start.3
  0.7 1.0 %copy-start = (bf16[512,512]{1,0:T(8,128)(2,1)S(1)}, bf16[512,512]{1,0:T(8,128)(2,1)}, u32[]{:S(2)}) copy-start(bf16[512,512]{1,0:T(8,128)(2,1)} %q_ref.1) | copy-start | bytes 1572868
  1.7 1.0 %copy-start.1 = (bf16[512,512]{1,0:T(8,128)(2,1)S(1)}, bf16[512,512]{1,0:T(8,128)(2,1)}, u32[]{:S(2)}) copy-start(bf16[512,512]{1,0:T(8,128)(2,1)} %k_ref.1) | copy-start | bytes 1572868
  2.8 1.0 %copy-start.2 = (bf16[512,512]{1,0:T(8,128)(2,1)S(1)}, bf16[512,512]{1,0:T(8,128)(2,1)}, u32[]{:S(2)}) copy-start(bf16[512,512]{1,0:T(8,128)(2,1)} %v_ref.1) | copy-start | bytes 1572868
